TPU v7x, 32 devices: a whole 2x2x4 slice. The times are simulated.
32 devices in a mesh: row: 4 (over x, core), col: 2 (over y), rep: 4 (over z).
Axes of the slice: x: 2, y: 2, z: 4, core: 2. Of those that a mesh axis runs over, the one named last changes fastest.
Arguments:
- vectors: float32 [8, 1024], P('rep', ('row', 'col')), may hold values from -6 to 6
- energies: float32 [1024], P(('row', 'col')), may hold values from 0 to 16
- tiles: bfloat16 [32, 128, 128], P(('row', 'col', 'rep')), may hold values from -0.375 to 0.375
- tile_codes: int32 [32], P(('row', 'col', 'rep')), may hold values from -1 to 7, as said below
Outputs:
- filtered: float32 [8, 1024], P('rep', ('row', 'col'))
- ritz_values: float32 [8], P('rep')
Inputs may be any that keep to these rules, and one draw needn't show every extreme that they name: `tile_codes`: slots of device (row, col, rep) hold tiles of grid cell (row, col) only. A code q stands for block row row * 2 + q // 4 and block column (q % 4) * 2 + col, which lies on or above the diagonal. Each cell holds its diagonal tile, each position at most once; a cell's tiles, in increasing code order, are dealt to its 4 devices in turn, so the occupied slots of a device come first and the rest are -1. Some device fills all 1 slots.
All inputs are finite; a program needn't handle non-finite values.
Results may differ from a plain program's by a relative error of at most 0.002.
Values may be sent and summed in bfloat16 or wider, within the bound.
A program may use at most 64 MiB of HBM per device.

v0:
```python
import jax
import jax.numpy as jnp
from jax import lax
from jax.sharding import PartitionSpec as P

filter_low = 5.0
filter_top = 20.0
spectrum_low = -3.0


def on_device(vectors, energies, tiles, tile_codes):
    rows_count = lax.axis_size("row")
    cols_count = lax.axis_size("col")
    reps_count = lax.axis_size("rep")
    row_index = lax.axis_index("row")
    col_index = lax.axis_index("col")
    tile_side = tiles.shape[1]
    local_count = vectors.shape[0]
    total_count = local_count * reps_count
    present = tile_codes >= 0
    safe_code = jnp.where(present, tile_codes, 0)
    block_row = safe_code // rows_count
    block_col = safe_code % rows_count
    on_diagonal = present & (block_row == col_index) & (block_col == row_index)
    upper_mask = lax.broadcasted_iota(jnp.int32, (tile_side, tile_side), 1) > lax.broadcasted_iota(
        jnp.int32, (tile_side, tile_side), 0
    )
    keep_mask = present[:, None, None] & (
        upper_mask[None] | jnp.logical_not(on_diagonal)[:, None, None]
    )
    stored = jnp.where(keep_mask, tiles, jnp.zeros((), tiles.dtype))
    row_select = jnp.where(
        present[:, None] & (block_row[:, None] == jnp.arange(cols_count)[None, :]), 1.0, 0.0
    ).astype(jnp.float32)
    col_select = jnp.where(
        present[:, None] & (block_col[:, None] == jnp.arange(rows_count)[None, :]), 1.0, 0.0
    ).astype(jnp.float32)

    def product(vector_block):
        rounded = vector_block.astype(jnp.bfloat16)[None]
        row_group = lax.all_gather(rounded, ("col", "rep"), axis=0, tiled=True).reshape(
            cols_count, total_count, tile_side
        )
        col_group = lax.all_gather(rounded, ("row", "rep"), axis=0, tiled=True).reshape(
            rows_count, total_count, tile_side
        )
        direct = jnp.einsum(
            "svj,sij->svi", col_group[block_col], stored, preferred_element_type=jnp.float32
        )
        mirror = jnp.einsum(
            "svi,sij->svj", row_group[block_row], stored, preferred_element_type=jnp.float32
        )
        row_terms = jnp.einsum("sa,svi->avi", row_select, direct, precision=lax.Precision.HIGHEST)
        col_terms = jnp.einsum("sk,svj->kvj", col_select, mirror, precision=lax.Precision.HIGHEST)
        row_total = lax.psum_scatter(
            row_terms.reshape(cols_count * reps_count, local_count, tile_side),
            ("col", "rep"),
            scatter_dimension=0,
            tiled=True,
        )[0]
        partial_rows = lax.psum_scatter(col_terms, "row", scatter_dimension=0, tiled=True)
        col_total = lax.psum_scatter(partial_rows, "rep", scatter_dimension=1, tiled=True)[0]
        return energies[None, :] * vector_block + row_total + col_total

    half = (filter_top - filter_low) / 2.0
    centre = (filter_top + filter_low) / 2.0
    sigma_first = half / (spectrum_low - centre)
    tau_value = 2.0 / sigma_first
    current = vectors
    previous = current
    latest = (product(current) - centre * current) * (sigma_first / half)
    sigma_next = 1.0 / (tau_value - sigma_first)
    newest = (product(latest) - centre * latest) * (
        2.0 * sigma_next / half
    ) - sigma_first * sigma_next * previous
    current = newest
    image = product(current)
    squares, crossed = lax.psum(
        (jnp.sum(current * current, axis=1), jnp.sum(current * image, axis=1)), ("row", "col")
    )
    ritz = crossed / (squares + 1e-06)
    resid = image - ritz[:, None] * current
    spacing = energies[None, :] - ritz[:, None]
    current = current - spacing / jnp.maximum(spacing * spacing, 1.0) * resid
    return (current, ritz)


def solution(mesh):
    in_specs = (
        P("rep", ("row", "col")),
        P(("row", "col")),
        P(("row", "col", "rep"), None, None),
        P(("row", "col", "rep")),
    )
    out_specs = (P("rep", ("row", "col")), P("rep"))
    return jax.shard_map(
        on_device, mesh=mesh, in_specs=in_specs, out_specs=out_specs, check_vma=False
    )
```

profile of v0, /device:TPU:0, one launch (start us, length us, event | category | flops | bytes accessed | tf_op | source)
XLA Modules:
  0.0 283.8 jit_solution(11361005302524389490)
XLA Ops:
  0.6 0.7 convert_bitcast_fusion.1
  1.3 22.1 %all-gather.7 = bf16[8,2,128]{2,1,0:T(2,128)(2,1)S(1)} all-gather(bf16[1,2,128]{2,1,0:T(2,128)(2,1)S(1)} %convert_bitcast_fusion.1), channel_id=3, replica_groups=mesh['row'=4,'col'=2,'rep'=4] {'col','rep'}, dimensions={0}, use_global_device_ids=true | all-gather | bytes 4608 | tf_op jit(solution)/shard_map/all_gather | solution.py:41
  24.2 0.7 copy-done.3
  25.1 10.1 %all-reduce.1 = f32[4,8,128]{2,1,0:T(8,128)S(1)} all-reduce(f32[4,8,128]{2,1,0:T(8,128)S(1)} %broadcast_multiply_fusion.2), channel_id=9, replica_groups=mesh['row'=4,'col'=2,'rep'=4] {'row'}, use_global_device_ids=true, to_apply=%region_1.2.clone | all-reduce | flops 4096 | bytes 32768
  35.2 0.7 copy-done.6
  35.9 0.6 dynamic-slice.26
  36.5 0.6 constant_dynamic-slice_fusion.7
  37.2 8.4 %all-reduce.2 = f32[1,8,128]{2,1,0:T(8,128)S(1)} all-reduce(f32[1,8,128]{2,1,0:T(8,128)S(1)} %constant_dynamic-slice_fusion.7), channel_id=10, replica_groups=mesh['row'=4,'col'=2,'rep'=4] {'rep'}, use_global_device_ids=true, to_apply=%region_2.3.clone | all-reduce | flops 1024 | bytes 8192
  45.6 0.6 dynamic-slice.28
  46.8 30.1 %all-gather.6 = bf16[16,2,128]{2,1,0:T(2,128)(2,1)S(1)} all-gather(bf16[1,2,128]{2,1,0:T(2,128)(2,1)S(1)} %convert_bitcast_fusion.1), channel_id=2, replica_groups=mesh['row'=4,'col'=2,'rep'=4] {'row','rep'}, dimensions={0}, use_global_device_ids=true | all-gather | bytes 8704 | tf_op jit(solution)/shard_map/all_gather | solution.py:44
  76.9 0.1 fusion.14
  77.2 17.9 %all-reduce = f32[8,2,128]{2,1,0:T(2,128)S(1)} all-reduce(f32[8,2,128]{2,1,0:T(2,128)S(1)} %bitcast.109), channel_id=8, replica_groups=mesh['row'=4,'col'=2,'rep'=4] {'col','rep'}, use_global_device_ids=true, to_apply=%region_0.1.clone | all-reduce | flops 2048 | bytes 16384
  95.1 0.6 dynamic-slice.24
  95.7 0.7 copy-done
  96.4 0.6 fusion.47
  97.0 17.8 %all-gather.9 = bf16[8,2,128]{2,1,0:T(2,128)(2,1)S(1)} all-gather(bf16[1,2,128]{2,1,0:T(2,128)(2,1)S(1)} %get-tuple-element.74), channel_id=5, replica_groups=mesh['row'=4,'col'=2,'rep'=4] {'col','rep'}, dimensions={0}, use_global_device_ids=true | all-gather | bytes 4608 | tf_op jit(solution)/shard_map/all_gather | solution.py:41
  115.1 10.1 %all-reduce.4 = f32[4,8,128]{2,1,0:T(8,128)S(1)} all-reduce(f32[4,8,128]{2,1,0:T(8,128)S(1)} %broadcast_multiply_fusion.1), channel_id=12, replica_groups=mesh['row'=4,'col'=2,'rep'=4] {'row'}, use_global_device_ids=true, to_apply=%region_4.5.clone | all-reduce | flops 4096 | bytes 32768
  125.2 0.6 constant_dynamic-slice_fusion.4
  125.8 8.7 %all-reduce.5 = f32[1,8,128]{2,1,0:T(8,128)S(1)} all-reduce(f32[1,8,128]{2,1,0:T(8,128)S(1)} %constant_dynamic-slice_fusion.4), channel_id=13, replica_groups=mesh['row'=4,'col'=2,'rep'=4] {'rep'}, use_global_device_ids=true, to_apply=%region_5.6.clone | all-reduce | flops 1024 | bytes 8192
  134.6 29.8 %all-gather.8 = bf16[16,2,128]{2,1,0:T(2,128)(2,1)S(1)} all-gather(bf16[1,2,128]{2,1,0:T(2,128)(2,1)S(1)} %get-tuple-element.74), channel_id=4, replica_groups=mesh['row'=4,'col'=2,'rep'=4] {'row','rep'}, dimensions={0}, use_global_device_ids=true | all-gather | bytes 8704 | tf_op jit(solution)/shard_map/all_gather | solution.py:44
  164.6 18.3 %all-reduce.3 = f32[8,2,128]{2,1,0:T(2,128)S(1)} all-reduce(f32[8,2,128]{2,1,0:T(2,128)S(1)} %bitcast.110), channel_id=11, replica_groups=mesh['row'=4,'col'=2,'rep'=4] {'col','rep'}, use_global_device_ids=true, to_apply=%region_3.4.clone | all-reduce | flops 2048 | bytes 16384
  182.9 0.6 convert_bitcast_fusion
  183.6 17.5 %all-gather.11 = bf16[8,2,128]{2,1,0:T(2,128)(2,1)S(1)} all-gather(bf16[1,2,128]{2,1,0:T(2,128)(2,1)S(1)} %get-tuple-element.72), channel_id=7, replica_groups=mesh['row'=4,'col'=2,'rep'=4] {'col','rep'}, dimensions={0}, use_global_device_ids=true | all-gather | bytes 4608 | tf_op jit(solution)/shard_map/all_gather | solution.py:41
  201.2 10.1 %all-reduce.7 = f32[4,8,128]{2,1,0:T(8,128)S(1)} all-reduce(f32[4,8,128]{2,1,0:T(8,128)S(1)} %broadcast_multiply_fusion), channel_id=15, replica_groups=mesh['row'=4,'col'=2,'rep'=4] {'row'}, use_global_device_ids=true, to_apply=%region_7.8.clone | all-reduce | flops 4096 | bytes 32768
  211.3 0.6 constant_dynamic-slice_fusion.1
  212.0 9.1 %all-reduce.8 = f32[1,8,128]{2,1,0:T(8,128)S(1)} all-reduce(f32[1,8,128]{2,1,0:T(8,128)S(1)} %constant_dynamic-slice_fusion.1), channel_id=16, replica_groups=mesh['row'=4,'col'=2,'rep'=4] {'rep'}, use_global_device_ids=true, to_apply=%region_8.9.clone | all-reduce | flops 1024 | bytes 8192
  221.1 29.4 %all-gather.10 = bf16[16,2,128]{2,1,0:T(2,128)(2,1)S(1)} all-gather(bf16[1,2,128]{2,1,0:T(2,128)(2,1)S(1)} %get-tuple-element.72), channel_id=6, replica_groups=mesh['row'=4,'col'=2,'rep'=4] {'row','rep'}, dimensions={0}, use_global_device_ids=true | all-gather | bytes 8704 | tf_op jit(solution)/shard_map/all_gather | solution.py:44
  250.5 0.1 fusion.6
  250.7 18.6 %all-reduce.6 = f32[8,2,128]{2,1,0:T(2,128)S(1)} all-reduce(f32[8,2,128]{2,1,0:T(2,128)S(1)} %bitcast.108), channel_id=14, replica_groups=mesh['row'=4,'col'=2,'rep'=4] {'col','rep'}, use_global_device_ids=true, to_apply=%region_6.7.clone | all-reduce | flops 2048 | bytes 16384
  269.3 0.7 multiply_reduce_fusion
  270.1 12.5 %all-reduce.9 = (f32[2]{0:T(128)S(1)}, f32[2]{0:T(128)S(1)}) all-reduce(f32[2]{0:T(128)S(1)} %get-tuple-element.69, f32[2]{0:T(128)S(1)} %get-tuple-element.68), channel_id=1, replica_groups=mesh['row'=4,'col'=2,'rep'=4] {'row','col'}, use_global_device_ids=true, to_apply=%region_10.11 | all-reduce | flops 4 | bytes 32 | tf_op jit(solution)/shard_map/psum | solution.py:78
  282.6 1.3 fusion.29
  (25 shorter events, 1.1 us)
Async XLA Ops:
  24.1 0.8 copy-start.3
  35.2 0.7 copy-start.6
  37.2 8.4 %copy-start.5 = (u32[32]{0:T(128)S(1)}, u32[32]{0:T(128)}, u32[]{:S(2)}) copy-start(u32[32]{0:T(128)} %constant.195) | copy-start | bytes 388
  77.2 17.9 %copy-start.4 = (u32[32]{0:T(128)S(1)}, u32[32]{0:T(128)}, u32[]{:S(2)}) copy-start(u32[32]{0:T(128)} %constant.187) | copy-start | bytes 388
  95.7 0.7 copy-start
  95.7 0.7 copy-start.1
  282.6 1.3 copy-start.2
where the time goes:
time: 284 us
  blocking collectives  271 us (95%)
  local copies, waits for them, and re-layouts  5.85 us (2%)
  other arithmetic  4.39 us (2%)
    unnamed x9, blocking collectives  111 us
    all_gather x3, blocking collectives, product(): lax.all_gather(rounded, ('row', 'rep'), axis=0, tiled=True)  89.4 us
    all_gather x3, blocking collectives, product(): lax.all_gather(rounded, ('col', 'rep'), axis=0, tiled=True)  57.5 us
    psum x1, blocking collectives, on_device(): lax.psum((jnp.sum(current * current, axis=1), jnp.sum(current * image, ax...  12.5 us
    unnamed x20, local copies, waits for them, and re-layouts  5.85 us

commit v1 on v0

--- a/solution.py
+++ b/solution.py
@@ -1,14 +1,281 @@
+import functools
+
 import jax
 import jax.numpy as jnp
 from jax import lax
+from jax.experimental import pallas as pl
+from jax.experimental.pallas import tpu as pltpu
 from jax.sharding import PartitionSpec as P
 
 filter_low = 5.0
 filter_top = 20.0
 spectrum_low = -3.0
 
-
-def on_device(vectors, energies, tiles, tile_codes):
+half = (filter_top - filter_low) / 2.0
+centre = (filter_top + filter_low) / 2.0
+sigma_first = half / (spectrum_low - centre)
+tau_value = 2.0 / sigma_first
+sigma_next = 1.0 / (tau_value - sigma_first)
+
+MESH = pl.DeviceIdType.MESH
+CODE_ROWS = 16
+
+
+def fused_kernel(
+    rows,
+    cols,
+    reps,
+    vectors_hbm,
+    energies_hbm,
+    tiles_hbm,
+    codes_hbm,
+    filtered_ref,
+    ritz_ref,
+    energies_ref,
+    raw_ref,
+    codes_ref,
+    pack_ref,
+    start_ref,
+    dense_ref,
+    state_ref,
+    part_ref,
+    local_sems,
+    pack_send,
+    pack_recv,
+    start_send,
+    start_recv,
+    part_send,
+    part_recv,
+):
+    row = lax.axis_index("row")
+    col = lax.axis_index("col")
+    rep = lax.axis_index("rep")
+    plane = rows * cols
+    place = row * cols + col
+    slots, side, _ = raw_ref.shape
+
+    def plane_peer(step):
+        other = lax.rem(place + step, plane)
+        return other, {"row": other // cols, "col": lax.rem(other, cols)}
+
+    def rep_peer(step):
+        other = lax.rem(rep + step, reps)
+        return other, {"rep": other}
+
+    barrier = pltpu.get_barrier_semaphore()
+    for step in range(1, reps):
+        pl.semaphore_signal(barrier, inc=1, device_id=rep_peer(step)[1], device_id_type=MESH)
+    for step in range(1, plane):
+        pl.semaphore_signal(barrier, inc=1, device_id=plane_peer(step)[1], device_id_type=MESH)
+
+    loads = [
+        pltpu.make_async_copy(codes_hbm, codes_ref, local_sems.at[0]),
+        pltpu.make_async_copy(tiles_hbm, raw_ref, local_sems.at[1]),
+        pltpu.make_async_copy(vectors_hbm, start_ref.at[place], local_sems.at[2]),
+        pltpu.make_async_copy(energies_hbm, energies_ref, local_sems.at[3]),
+    ]
+    for load in loads:
+        load.start()
+    loads[0].wait()
+    loads[1].wait()
+    line = lax.broadcasted_iota(jnp.int32, (side, side), 0)
+    lane = lax.broadcasted_iota(jnp.int32, (side, side), 1)
+    diagonal_code = col * rows + row
+    for slot in range(slots):
+        code = jnp.full((side, side), codes_ref[slot], jnp.int32)
+        keep = (code >= 0) & ((lane > line) | (code != diagonal_code))
+        tile = jnp.where(keep, raw_ref[slot].astype(jnp.float32), 0.0)
+        pack_ref[rep, slot, :side] = tile.astype(jnp.bfloat16)
+        pack_ref[rep, slot, side:] = code[:CODE_ROWS].astype(jnp.float32).astype(jnp.bfloat16)
+    loads[2].wait()
+    loads[3].wait()
+    pl.semaphore_wait(barrier, reps - 1 + plane - 1)
+
+    sends = []
+    for step in range(1, reps):
+        other, device = rep_peer(step)
+        copy = pltpu.make_async_remote_copy(
+            src_ref=pack_ref.at[rep],
+            dst_ref=pack_ref.at[rep],
+            send_sem=pack_send.at[step],
+            recv_sem=pack_recv.at[rep],
+            device_id=device,
+            device_id_type=MESH,
+        )
+        copy.start()
+        sends.append(copy)
+
+    def spread(buffer, send_sems, recv_sems):
+        for step in range(1, plane):
+            other, device = plane_peer(step)
+            copy = pltpu.make_async_remote_copy(
+                src_ref=buffer.at[place],
+                dst_ref=buffer.at[place],
+                send_sem=send_sems.at[step],
+                recv_sem=recv_sems.at[place],
+                device_id=device,
+                device_id_type=MESH,
+            )
+            copy.start()
+            sends.append(copy)
+
+    def collect(buffer, recv_sems):
+        for step in range(1, plane):
+            other, device = plane_peer(step)
+            pltpu.make_async_remote_copy(
+                src_ref=buffer.at[other],
+                dst_ref=buffer.at[other],
+                send_sem=recv_sems.at[other],
+                recv_sem=recv_sems.at[other],
+                device_id=device,
+                device_id_type=MESH,
+            ).wait_recv()
+
+    spread(start_ref, start_send, start_recv)
+
+    def place_tiles(source, first):
+        for slot in range(slots):
+            tile = pack_ref[source, slot, :side].reshape(side // CODE_ROWS, CODE_ROWS, side)
+            code = pack_ref[source, slot, side:].astype(jnp.float32)
+            for a in range(cols):
+                for k in range(rows):
+                    spot = jnp.where(code == float(a * rows + k), 1.0, 0.0).astype(jnp.bfloat16)
+                    term = (tile * spot[None]).reshape(side, side)
+                    here = (pl.ds(a * side, side), pl.ds(k * side, side))
+                    if first and slot == 0:
+                        dense_ref[here] = term
+                    else:
+                        dense_ref[here] = dense_ref[here] + term
+
+    place_tiles(rep, True)
+    collect(start_ref, start_recv)
+    for step in range(1, reps):
+        other, device = rep_peer(step)
+        pltpu.make_async_remote_copy(
+            src_ref=pack_ref.at[other],
+            dst_ref=pack_ref.at[other],
+            send_sem=pack_recv.at[other],
+            recv_sem=pack_recv.at[other],
+            device_id=device,
+            device_id_type=MESH,
+        ).wait_recv()
+        place_tiles(other, False)
+
+    energies = energies_ref[...]
+
+    def product(phase, state, scale, own_term):
+        column_part = jnp.concatenate([state[k * cols + col] for k in range(rows)], axis=1)
+        row_part = jnp.concatenate([state[row * cols + a] for a in range(cols)], axis=1)
+        direct = lax.dot_general(
+            column_part.astype(jnp.bfloat16),
+            dense_ref[...],
+            (((1,), (1,)), ((), ())),
+            preferred_element_type=jnp.float32,
+        )
+        mirror = lax.dot_general(
+            row_part.astype(jnp.bfloat16),
+            dense_ref[...],
+            (((1,), (0,)), ((), ())),
+            preferred_element_type=jnp.float32,
+        )
+        buffer = part_ref.at[phase]
+        for a in range(cols):
+            owned = jnp.where(col == a, own_term, 0.0)
+            buffer[place, a] = direct[:, a * side : (a + 1) * side] * scale + owned
+        for k in range(rows):
+            buffer[place, cols + k] = mirror[:, k * side : (k + 1) * side] * scale
+        spread(buffer, part_send.at[phase], part_recv.at[phase])
+        collect(buffer, part_recv.at[phase])
+        totals = []
+        for block in range(plane):
+            terms = []
+            for c in range(cols):
+                terms.append(buffer[(block // cols) * cols + c, block % cols])
+            for r in range(rows):
+                terms.append(buffer[r * cols + block % cols, cols + block // cols])
+            total = terms[0]
+            for term in terms[1:]:
+                total = total + term
+            totals.append(total)
+        return totals
+
+    scale = sigma_first / half
+    start_own = start_ref[place]
+    latest = product(0, start_ref, scale, (energies * start_own - centre * start_own) * scale)
+    for block in range(plane):
+        state_ref[0, block] = latest[block]
+    scale = 2.0 * sigma_next / half
+    own = state_ref[0, place]
+    newest = product(
+        1,
+        state_ref.at[0],
+        scale,
+        (energies * own - centre * own) * scale - sigma_first * sigma_next * start_own,
+    )
+    for block in range(plane):
+        state_ref[1, block] = newest[block]
+    own = state_ref[1, place]
+    image = product(2, state_ref.at[1], 1.0, energies * own)
+    for block in range(plane):
+        state_ref[2, block] = image[block]
+    squares = newest[0] * newest[0]
+    crossed = newest[0] * image[0]
+    for block in range(1, plane):
+        squares = squares + newest[block] * newest[block]
+        crossed = crossed + newest[block] * image[block]
+    ritz = jnp.sum(crossed, axis=1, keepdims=True) / (
+        jnp.sum(squares, axis=1, keepdims=True) + 1e-06
+    )
+    resid = state_ref[2, place] - ritz * own
+    spacing = energies - ritz
+    filtered_ref[...] = own - spacing / jnp.maximum(spacing * spacing, 1.0) * resid
+    for vector in range(own.shape[0]):
+        ritz_ref[vector] = ritz[vector, 0]
+    for copy in sends:
+        copy.wait_send()
+
+
+def fused(vectors, energies, tiles, tile_codes):
+    rows = lax.axis_size("row")
+    cols = lax.axis_size("col")
+    reps = lax.axis_size("rep")
+    plane = rows * cols
+    local_count = vectors.shape[0]
+    slots, side, _ = tiles.shape
+    vector_shape = (local_count, side)
+    return pl.pallas_call(
+        functools.partial(fused_kernel, rows, cols, reps),
+        out_shape=(
+            jax.ShapeDtypeStruct(vector_shape, jnp.float32),
+            jax.ShapeDtypeStruct((local_count,), jnp.float32),
+        ),
+        in_specs=[pl.BlockSpec(memory_space=pl.ANY)] * 4,
+        out_specs=(
+            pl.BlockSpec(memory_space=pltpu.VMEM),
+            pl.BlockSpec(memory_space=pltpu.SMEM),
+        ),
+        scratch_shapes=[
+            pltpu.VMEM((1, side), jnp.float32),
+            pltpu.VMEM((slots, side, side), jnp.bfloat16),
+            pltpu.SMEM((slots,), jnp.int32),
+            pltpu.VMEM((reps, slots, side + CODE_ROWS, side), jnp.bfloat16),
+            pltpu.VMEM((plane,) + vector_shape, jnp.float32),
+            pltpu.VMEM((cols * side, rows * side), jnp.bfloat16),
+            pltpu.VMEM((3, plane) + vector_shape, jnp.float32),
+            pltpu.VMEM((3, plane, cols + rows) + vector_shape, jnp.float32),
+            pltpu.SemaphoreType.DMA((4,)),
+            pltpu.SemaphoreType.DMA((reps,)),
+            pltpu.SemaphoreType.DMA((reps,)),
+            pltpu.SemaphoreType.DMA((plane,)),
+            pltpu.SemaphoreType.DMA((plane,)),
+            pltpu.SemaphoreType.DMA((3, plane)),
+            pltpu.SemaphoreType.DMA((3, plane)),
+        ],
+        compiler_params=pltpu.CompilerParams(collective_id=0, has_side_effects=True),
+    )(vectors, energies.reshape(1, side), tiles, tile_codes)
+
+
+def collective_form(vectors, energies, tiles, tile_codes):
     rows_count = lax.axis_size("row")
     cols_count = lax.axis_size("col")
     reps_count = lax.axis_size("rep")
@@ -36,6 +303,15 @@
         present[:, None] & (block_col[:, None] == jnp.arange(rows_count)[None, :]), 1.0, 0.0
     ).astype(jnp.float32)
 
+    def chosen(select, group):
+        picked = jnp.einsum(
+            "sk,kvj->svj",
+            select.astype(group.dtype),
+            group,
+            preferred_element_type=jnp.float32,
+        )
+        return picked.astype(group.dtype)
+
     def product(vector_block):
         rounded = vector_block.astype(jnp.bfloat16)[None]
         row_group = lax.all_gather(rounded, ("col", "rep"), axis=0, tiled=True).reshape(
@@ -45,10 +321,10 @@
             rows_count, total_count, tile_side
         )
         direct = jnp.einsum(
-            "svj,sij->svi", col_group[block_col], stored, preferred_element_type=jnp.float32
+            "svj,sij->svi", chosen(col_select, col_group), stored, preferred_element_type=jnp.float32
         )
         mirror = jnp.einsum(
-            "svi,sij->svj", row_group[block_row], stored, preferred_element_type=jnp.float32
+            "svi,sij->svj", chosen(row_select, row_group), stored, preferred_element_type=jnp.float32
         )
         row_terms = jnp.einsum("sa,svi->avi", row_select, direct, precision=lax.Precision.HIGHEST)
         col_terms = jnp.einsum("sk,svj->kvj", col_select, mirror, precision=lax.Precision.HIGHEST)
@@ -85,6 +361,14 @@
     return (current, ritz)
 
 
+def on_device(vectors, energies, tiles, tile_codes):
+    plane = lax.axis_size("row") * lax.axis_size("col")
+    placed = lax.axis_size("rep") * tiles.shape[0] * plane
+    if placed <= 256 and energies.shape[0] == tiles.shape[1]:
+        return fused(vectors, energies, tiles, tile_codes)
+    return collective_form(vectors, energies, tiles, tile_codes)
+
+
 def solution(mesh):
     in_specs = (
         P("rep", ("row", "col")),

time: 284 us -> 24.7 us (0.09)
  blocking collectives: 271 us -> 0 us
  Pallas kernels: 0 us -> 21.3 us
  other arithmetic: 4.39 us -> 0 us
  local copies, waits for them, and re-layouts: 5.85 us -> 1.8 us
    all_gather x6 -> x0, blocking collectives: 147 us -> none  [the longest x3 89.4 us: product(): lax.all_gather(rounded, ('row', 'rep'), axis=0, tiled=True)]
    unnamed x9 -> x0, blocking collectives: 111 us -> none
    pallas_call x0 -> x1, Pallas kernels: none -> 21.3 us  [fused(): pl.pallas_call(functools.partial(fused_kernel, rows, cols, reps), out_sha...]
    psum x1 -> x0, blocking collectives: 12.5 us -> none  [on_device(): lax.psum((jnp.sum(current * current, axis=1), jnp.sum(current * image, ax...]
    unnamed x20 -> x6, local copies, waits for them, and re-layouts: 5.85 us -> 1.8 us
where the time goes in v1:
time: 24.7 us; the launch traced here: 24.4 us
  Pallas kernels  21.3 us (86%)
  local copies, waits for them, and re-layouts  1.8 us (7%)
  between operations  1.29 us (5%)
    pallas_call x1, Pallas kernels, fused(): pl.pallas_call(functools.partial(fused_kernel, rows, cols, reps), out_sha...  21.3 us
    unnamed x6, local copies, waits for them, and re-layouts  1.8 us

profile of v1, /device:TPU:0, one launch (start us, length us, event | category | flops | bytes accessed | tf_op | source)
XLA Modules:
  0.0 24.4 jit_solution(5166264972128482623)
XLA Ops:
  1.3 21.3 %shard_map.59 = (f32[2,128]{1,0:T(2,128)}, f32[2]{0:T(128)}) custom-call(f32[2,128]{1,0:T(2,128)} %vectors_hbm.1, f32[1,128]{1,0:T(1,128)} %bitcast.1, bf16[1,128,128]{2,1,0:T(8,128)(2,1)} %tiles_hbm.1, s32[1]{0:T(128)S(6)} %copy.8.codes_hbm), custom_call_target="tpu_custom_call" | custom-call | tf_op jit(solution)/shard_map/pallas_call | solution.py:246
  22.6 0.0 copy-start
  22.6 0.7 %copy-done = f32[2,128]{1,0:T(2,128)S(1)} copy-done((f32[2,128]{1,0:T(2,128)S(1)}, f32[2,128]{1,0:T(2,128)}, u32[]{:S(2)}) %copy-start) | copy-done | bytes 1048
  23.3 0.0 copy-start.1
  23.3 0.6 %copy.9 = f32[2,128]{1,0:T(2,128)} copy(f32[2,128]{1,0:T(2,128)S(1)} %copy-done) | data formatting | bytes 2048
  23.9 0.1 copy-done.1
  23.9 0.5 %copy.10 = f32[2]{0:T(128)} copy(f32[2]{0:T(128)S(1)} %copy-done.1) | data formatting | bytes 16
Async XLA Ops:
  22.6 0.7 %copy-start = (f32[2,128]{1,0:T(2,128)S(1)}, f32[2,128]{1,0:T(2,128)}, u32[]{:S(2)}) copy-start(f32[2,128]{1,0:T(2,128)} %get-tuple-element.4) | copy-start | bytes 3076
  23.3 0.6 %copy-start.1 = (f32[2]{0:T(128)S(1)}, f32[2]{0:T(128)}, u32[]{:S(2)}) copy-start(f32[2]{0:T(128)} %get-tuple-element.5) | copy-start | bytes 28

commit v2 on v1

--- a/solution.py
+++ b/solution.py
@@ -29,8 +29,7 @@
     energies_hbm,
     tiles_hbm,
     codes_hbm,
-    filtered_ref,
-    ritz_ref,
+    result_ref,
     energies_ref,
     raw_ref,
     codes_ref,
@@ -228,9 +227,8 @@
     )
     resid = state_ref[2, place] - ritz * own
     spacing = energies - ritz
-    filtered_ref[...] = own - spacing / jnp.maximum(spacing * spacing, 1.0) * resid
-    for vector in range(own.shape[0]):
-        ritz_ref[vector] = ritz[vector, 0]
+    result_ref[0] = own - spacing / jnp.maximum(spacing * spacing, 1.0) * resid
+    result_ref[1] = jnp.broadcast_to(ritz, own.shape)
     for copy in sends:
         copy.wait_send()
 
@@ -243,17 +241,11 @@
     local_count = vectors.shape[0]
     slots, side, _ = tiles.shape
     vector_shape = (local_count, side)
-    return pl.pallas_call(
+    result = pl.pallas_call(
         functools.partial(fused_kernel, rows, cols, reps),
-        out_shape=(
-            jax.ShapeDtypeStruct(vector_shape, jnp.float32),
-            jax.ShapeDtypeStruct((local_count,), jnp.float32),
-        ),
+        out_shape=pltpu.VMEM((2,) + vector_shape, jnp.float32),
         in_specs=[pl.BlockSpec(memory_space=pl.ANY)] * 4,
-        out_specs=(
-            pl.BlockSpec(memory_space=pltpu.VMEM),
-            pl.BlockSpec(memory_space=pltpu.SMEM),
-        ),
+        out_specs=pl.BlockSpec(memory_space=pltpu.VMEM),
         scratch_shapes=[
             pltpu.VMEM((1, side), jnp.float32),
             pltpu.VMEM((slots, side, side), jnp.bfloat16),
@@ -273,6 +265,7 @@
         ],
         compiler_params=pltpu.CompilerParams(collective_id=0, has_side_effects=True),
     )(vectors, energies.reshape(1, side), tiles, tile_codes)
+    return result[0], result[1, :, 0]
 
 
 def collective_form(vectors, energies, tiles, tile_codes):

time: 24.7 us -> 23.4 us (0.947)
  local copies, waits for them, and re-layouts: 1.8 us -> 1.19 us
  Pallas kernels: 21.3 us -> 20.7 us
    unnamed x6 -> x0, local copies, waits for them, and re-layouts: 1.8 us -> none
    slice x0 -> x1, local copies, waits for them, and re-layouts: none -> 0.63 us  [fused(): return (result[0], result[1, :, 0])]
    pallas_call x1, Pallas kernels: 21.3 us -> 20.7 us  [fused(): pl.pallas_call(functools.partial(fused_kernel, rows, cols, reps), out_sha...]
    squeeze x0 -> x1, local copies, waits for them, and re-layouts: none -> 0.56 us  [fused(): return (result[0], result[1, :, 0])]
where the time goes in v2:
time: 23.4 us; the launch traced here: 23.2 us
  Pallas kernels  20.7 us (88%)
  between operations  1.29 us (6%)
  local copies, waits for them, and re-layouts  1.19 us (5%)
    pallas_call x1, Pallas kernels, fused(): pl.pallas_call(functools.partial(fused_kernel, rows, cols, reps), out_sha...  20.7 us
    slice x1, local copies, waits for them, and re-layouts, fused(): return (result[0], result[1, :, 0])  0.63 us
    squeeze x1, local copies, waits for them, and re-layouts, fused(): return (result[0], result[1, :, 0])  0.56 us

profile of v2, /device:TPU:0, one launch (start us, length us, event | category | flops | bytes accessed | tf_op | source)
XLA Modules:
  0.0 23.2 jit_solution(16621834818939384599)
XLA Ops:
  1.3 20.7 %shard_map.59 = f32[2,2,128]{2,1,0:T(2,128)S(1)} custom-call(f32[2,128]{1,0:T(2,128)} %vectors_hbm.1, f32[1,128]{1,0:T(1,128)} %bitcast.3, bf16[1,128,128]{2,1,0:T(8,128)(2,1)} %tiles_hbm.1, s32[1]{0:T(128)S(6)} %copy.6.codes_hbm), custom_call_target="tpu_custom_call" | custom-call | tf_op jit(solution)/shard_map/pallas_call | solution.py:244
  22.0 0.6 %slice_reduce_fusion = f32[2]{0:T(128)} fusion(f32[2,2,128]{2,1,0:T(2,128)S(1)} %shard_map.59), kind=kLoop, calls=%fused_computation | loop fusion | bytes 16 | tf_op jit(solution)/shard_map/slice | solution.py:268
  22.6 0.6 %slice_bitcast_fusion = f32[2,128]{1,0:T(2,128)} fusion(f32[2,2,128]{2,1,0:T(2,128)S(1)} %shard_map.59), kind=kLoop, calls=%fused_computation.1 | loop fusion | bytes 2048 | tf_op jit(solution)/shard_map/squeeze | solution.py:268

commit v3 on v2

--- a/solution.py
+++ b/solution.py
@@ -231,6 +231,12 @@
     result_ref[1] = jnp.broadcast_to(ritz, own.shape)
     for copy in sends:
         copy.wait_send()
+
+
+def output_kernel(result_ref, filtered_ref, ritz_ref):
+    filtered_ref[...] = result_ref[0]
+    for vector in range(ritz_ref.shape[0]):
+        ritz_ref[vector] = result_ref[1, vector, 0]
 
 
 def fused(vectors, energies, tiles, tile_codes):
@@ -265,7 +271,18 @@
         ],
         compiler_params=pltpu.CompilerParams(collective_id=0, has_side_effects=True),
     )(vectors, energies.reshape(1, side), tiles, tile_codes)
-    return result[0], result[1, :, 0]
+    return pl.pallas_call(
+        output_kernel,
+        out_shape=(
+            jax.ShapeDtypeStruct(vector_shape, jnp.float32),
+            jax.ShapeDtypeStruct((local_count,), jnp.float32),
+        ),
+        in_specs=[pl.BlockSpec(memory_space=pltpu.VMEM)],
+        out_specs=(
+            pl.BlockSpec(memory_space=pltpu.VMEM),
+            pl.BlockSpec(memory_space=pltpu.SMEM),
+        ),
+    )(pltpu.with_memory_space_constraint(result, pltpu.VMEM))
 
 
 def collective_form(vectors, energies, tiles, tile_codes):

time: 23.4 us -> 22.8 us (0.974)
  local copies, waits for them, and re-layouts: 1.19 us -> 0 us
  Pallas kernels: 20.7 us -> 21.3 us
    slice x1 -> x0, local copies, waits for them, and re-layouts: 0.63 us -> none  [fused(): return (result[0], result[1, :, 0])]
    pallas_call x0 -> x1, Pallas kernels: none -> 0.57 us  [fused(): pl.pallas_call(output_kernel, out_shape=(jax.ShapeDtypeStruct(vector_shap...]
    squeeze x1 -> x0, local copies, waits for them, and re-layouts: 0.56 us -> none  [fused(): return (result[0], result[1, :, 0])]
where the time goes in v3:
time: 22.8 us; the launch traced here: 22.6 us
  Pallas kernels  21.3 us (93%)
  between operations  1.28 us (6%)
    pallas_call x1, Pallas kernels, fused(): pl.pallas_call(functools.partial(fused_kernel, rows, cols, reps), out_sha...  20.7 us
    pallas_call x1, Pallas kernels, fused(): pl.pallas_call(output_kernel, out_shape=(jax.ShapeDtypeStruct(vector_shap...  0.57 us

profile of v3, /device:TPU:0, one launch (start us, length us, event | category | flops | bytes accessed | tf_op | source)
XLA Modules:
  0.0 22.6 jit_solution(8622372013090216742)
XLA Ops:
  1.3 20.7 %shard_map.59.result_ref = f32[2,2,128]{2,1,0:T(2,128)S(1)} custom-call(f32[2,128]{1,0:T(2,128)} %vectors_hbm.1, f32[1,128]{1,0:T(1,128)} %bitcast.1, bf16[1,128,128]{2,1,0:T(8,128)(2,1)} %tiles_hbm.1, s32[1]{0:T(128)S(6)} %copy.6.codes_hbm), custom_call_target="tpu_custom_call" | custom-call | tf_op jit(solution)/shard_map/pallas_call | solution.py:250
  22.0 0.6 %shard_map.60 = (f32[2,128]{1,0:T(2,128)}, f32[2]{0:T(128)}) custom-call(f32[2,2,128]{2,1,0:T(2,128)S(1)} %shard_map.59.result_ref), custom_call_target="tpu_custom_call" | custom-call | tf_op jit(solution)/shard_map/pallas_call | solution.py:274

commit v4 on v3

--- a/solution.py
+++ b/solution.py
@@ -86,8 +86,6 @@
         tile = jnp.where(keep, raw_ref[slot].astype(jnp.float32), 0.0)
         pack_ref[rep, slot, :side] = tile.astype(jnp.bfloat16)
         pack_ref[rep, slot, side:] = code[:CODE_ROWS].astype(jnp.float32).astype(jnp.bfloat16)
-    loads[2].wait()
-    loads[3].wait()
     pl.semaphore_wait(barrier, reps - 1 + plane - 1)
 
     sends = []
@@ -130,6 +128,7 @@
                 device_id_type=MESH,
             ).wait_recv()
 
+    loads[2].wait()
     spread(start_ref, start_send, start_recv)
 
     def place_tiles(source, first):
@@ -160,6 +159,7 @@
         ).wait_recv()
         place_tiles(other, False)
 
+    loads[3].wait()
     energies = energies_ref[...]
 
     def product(phase, state, scale, own_term):

time: 22.8 us -> 22.8 us (level)
  no operation moved by 1% of the time
where the time goes in v4:
time: 22.8 us; the launch traced here: 22.6 us
  Pallas kernels  21.3 us (93%)
  between operations  1.28 us (6%)
    pallas_call x1, Pallas kernels, fused(): pl.pallas_call(functools.partial(fused_kernel, rows, cols, reps), out_sha...  20.8 us
    pallas_call x1, Pallas kernels, fused(): pl.pallas_call(output_kernel, out_shape=(jax.ShapeDtypeStruct(vector_shap...  0.57 us

profile of v4, /device:TPU:0, one launch (start us, length us, event | category | flops | bytes accessed | tf_op | source)
XLA Modules:
  0.0 22.6 jit_solution(1213528048187452156)
XLA Ops:
  1.3 20.8 %shard_map.59.result_ref = f32[2,2,128]{2,1,0:T(2,128)S(1)} custom-call(f32[2,128]{1,0:T(2,128)} %vectors_hbm.1, f32[1,128]{1,0:T(1,128)} %bitcast.1, bf16[1,128,128]{2,1,0:T(8,128)(2,1)} %tiles_hbm.1, s32[1]{0:T(128)S(6)} %copy.6.codes_hbm), custom_call_target="tpu_custom_call" | custom-call | tf_op jit(solution)/shard_map/pallas_call | solution.py:250
  22.0 0.6 %shard_map.60 = (f32[2,128]{1,0:T(2,128)}, f32[2]{0:T(128)}) custom-call(f32[2,2,128]{2,1,0:T(2,128)S(1)} %shard_map.59.result_ref), custom_call_target="tpu_custom_call" | custom-call | tf_op jit(solution)/shard_map/pallas_call | solution.py:274
